TPU v7x, 32 devices: a whole 2x2x4 slice. The times are simulated.
32 devices in a mesh: groups: 2 (over x), orient: 8 (over z, y), img: 2 (over core).
Axes of the slice: x: 2, y: 2, z: 4, core: 2. Of those that a mesh axis runs over, the one named last changes fastest.
Arguments:
- images: bfloat16 [256, 16384], P(('groups', 'orient', 'img')), parts along dimension 0, may hold values from -600 to 600
- image_shift: int32 [256, 2], P(('groups', 'orient', 'img')), parts along dimension 0, may hold values from -4 to 4
- image_group: int32 [256], P(('groups', 'orient', 'img')), parts along dimension 0, may hold values from 0 to 7
- projections: bfloat16 [2816, 16384], P(('orient', 'img')), may hold values from -0.48 to 0.48
- slice_class: int32 [2816], P(('orient', 'img')), may hold values from 0 to 23
- slice_angle: int32 [2816], P(('orient', 'img')), may hold values from 0 to 4607
- log_prior: float32 [24, 4608], replicated, may hold values from -3 to 0
- ctf_table: float32 [8, 8192], replicated, may hold values from -1 to 1
Outputs:
- weighted_sums: bfloat16 [5632, 16384], P(('groups', 'orient', 'img')), parts along dimension 0
- group_mass: float32 [8, 5632], P(None, ('groups', 'orient', 'img')), parts along dimension 1
- class_posterior: float32 [256, 24], P(('groups', 'orient', 'img')), parts along dimension 0
- log_evidence: float32 [256], P(('groups', 'orient', 'img')), parts along dimension 0
There are 2 independent parts, one for each index of `groups`. A program takes and returns all parts, laid end to end along the dimension named above; an argument that names none is the same for every part. Nothing has to cross between parts.
All inputs are finite; a program needn't handle non-finite values.
Results may differ from a plain program's by a relative error of at most 0.0045.
Values may be sent and summed in bfloat16 or wider, within the bound.
A program may use at most 128 MiB of HBM per device.

v0:
```python
import math

import jax
import jax.numpy as jnp
from jax import lax
from jax.sharding import PartitionSpec as P

KY = 128
KX = 64
HALF = 8192
CLASSES = 24
ORIENTS = 4608
GROUPS = 8
BOX = 128


def prepare_rows(images, image_shift, contrast):
    row_count = images.shape[0]
    real_part = images[:, :HALF].astype(jnp.float32)
    imag_part = images[:, HALF:].astype(jnp.float32)
    freq_y = (jnp.arange(KY, dtype=jnp.int32) - KY // 2).astype(jnp.float32)
    freq_x = jnp.arange(KX, dtype=jnp.int32).astype(jnp.float32)
    shift_x = image_shift[:, 0].astype(jnp.float32)
    shift_y = image_shift[:, 1].astype(jnp.float32)
    phases = (
        2.0
        * math.pi
        / BOX
        * (
            shift_y[:, None, None] * freq_y[None, :, None]
            + shift_x[:, None, None] * freq_x[None, None, :]
        )
    )
    phases = phases.reshape(row_count, HALF)
    cosine = jnp.cos(phases)
    sine_part = jnp.sin(phases)
    moved_real = contrast * (real_part * cosine + imag_part * sine_part)
    moved_imag = contrast * (imag_part * cosine - real_part * sine_part)
    return jnp.concatenate([moved_real, moved_imag], axis=1).astype(jnp.bfloat16)


def one_hot_groups(group_ids):
    return (group_ids[:, None] == jnp.arange(GROUPS, dtype=jnp.int32)[None, :]).astype(jnp.float32)


def body(
    images, image_shift, image_group, projections, slice_class, slice_angle, log_prior, ctf_table
):
    rows_local = images.shape[0]
    contrast = jnp.dot(one_hot_groups(image_group), ctf_table, precision=lax.Precision.HIGHEST)
    prepared = prepare_rows(images, image_shift, contrast)
    squared_ctf = ctf_table * ctf_table
    prior_row = jnp.take(log_prior.reshape(-1), slice_class * ORIENTS + slice_angle)
    class_hot = (slice_class[:, None] == jnp.arange(CLASSES, dtype=jnp.int32)[None, :]).astype(
        jnp.float32
    )
    real_block = projections[:, :HALF].astype(jnp.float32)
    imag_block = projections[:, HALF:].astype(jnp.float32)
    powers = real_block * real_block + imag_block * imag_block
    per_group = jnp.dot(squared_ctf, powers.T, precision=lax.Precision.HIGHEST)
    gathered, groups_all = (
        lax.all_gather(prepared, ("orient", "img"), axis=0, tiled=True),
        lax.all_gather(image_group, ("orient", "img"), axis=0, tiled=True),
    )
    raw = lax.dot_general(
        gathered, projections, (((1,), (1,)), ((), ())), preferred_element_type=jnp.float32
    )
    self_terms = jnp.dot(one_hot_groups(groups_all), per_group, precision=lax.Precision.HIGHEST)
    scores = raw - 0.5 * self_terms + prior_row[None, :]
    first_row = lax.axis_index(("orient", "img")) * rows_local
    maxima = lax.pmax(jnp.max(scores, axis=1), ("orient", "img"))
    exponent = jnp.exp(scores - maxima[:, None])
    totals = lax.psum(jnp.sum(exponent, axis=1), ("orient", "img"))
    class_own = lax.psum_scatter(
        jnp.dot(exponent, class_hot, precision=lax.Precision.HIGHEST),
        ("orient", "img"),
        scatter_dimension=0,
        tiled=True,
    )
    weights = (exponent / totals[:, None]).astype(jnp.bfloat16)
    summed = lax.dot_general(
        weights, gathered, (((0,), (0,)), ((), ())), preferred_element_type=jnp.float32
    )
    masses = lax.dot_general(
        one_hot_groups(groups_all).astype(jnp.bfloat16),
        weights,
        (((0,), (0,)), ((), ())),
        preferred_element_type=jnp.float32,
    )
    summed_out = summed.astype(jnp.bfloat16)
    totals_own = lax.dynamic_slice_in_dim(totals, first_row, rows_local, 0)
    maxima_own = lax.dynamic_slice_in_dim(maxima, first_row, rows_local, 0)
    class_posterior = class_own / totals_own[:, None]
    log_evidence = maxima_own + jnp.log(totals_own)
    return (summed_out, masses, class_posterior, log_evidence)


def solution(mesh):
    in_specs = (
        P(("groups", "orient", "img"), None),
        P(("groups", "orient", "img"), None),
        P(("groups", "orient", "img")),
        P(("orient", "img"), None),
        P(("orient", "img")),
        P(("orient", "img")),
        P(),
        P(),
    )
    out_specs = (
        P(("groups", "orient", "img"), None),
        P(None, ("groups", "orient", "img")),
        P(("groups", "orient", "img"), None),
        P(("groups", "orient", "img")),
    )
    return jax.shard_map(body, mesh=mesh, in_specs=in_specs, out_specs=out_specs, check_vma=False)
```

profile of v0, /device:TPU:0, one launch (start us, length us, event | category | flops | bytes accessed | tf_op | source)
XLA Modules:
  0.0 177.3 jit_solution(11477995381683493264)
XLA Ops:
  7.2 0.0 copy-start
  7.2 0.0 all-gather.2.cloned.1.call-start
  7.2 0.8 convert_bitcast_fusion.1
  8.0 0.1 broadcast_multiply_fusion.1
  8.1 0.1 broadcast_multiply_fusion
  8.1 1.9 %fusion.11 = (f32[8,128,64]{2,1,0:T(8,128)S(1)}, f32[8,128,64]{2,1,0:T(8,128)S(1)}) fusion(f32[8,64]{1,0:T(8,128)S(1)} %broadcast_multiply_fusion, f32[8,128]{1,0:T(8,128)S(1)} %broadcast_multiply_fusion.1), kind=kLoop, calls=%fused_computation.15 | loop fusion | flops 131072 | bytes 530432 | tf_op jit(solution)/shard_map/cos | solution.py:35
  10.1 0.2 cos.7
  10.2 0.2 sin.7
  10.4 1.4 fusion.14
  11.8 0.7 pad_maximum_fusion
  12.6 0.0 all-gather.2.cloned.1.call-update
  12.6 1.0 reshape.117
  13.7 1.3 fusion.28
  16.3 0.9 dynamic-update-slice
  17.1 0.7 compare_select_fusion
  17.9 1.4 gather_fusion
  19.3 13.9 %all-reduce = s32[128]{0:T(128)S(1)} all-reduce(s32[128]{0:T(128)S(1)} %dynamic-update-slice), channel_id=1, replica_groups=mesh['groups'=2,'orient'=8,'img'=2] {'orient','img'}, use_global_device_ids=true, to_apply=%add | all-reduce | flops 128 | bytes 1024
  33.2 0.0 copy-done
  33.2 6.6 %fusion = f32[8,176]{1,0:T(8,128)S(1)} fusion(bf16[176,16384]{1,0:T(8,128)(2,1)} %param.11, f32[8,8192]{1,0:T(8,128)S(1)} %copy-done), kind=kOutput, calls=%fused_computation.2 | convolution fusion | flops 145686528 | bytes 6034944 | tf_op jit(solution)/shard_map/dot_general | solution.py:60
  39.8 0.0 copy-start.1
  39.8 26.4 %all-gather.2.cloned.1.call-done = bf16[128,16384]{1,0:T(8,128)(2,1)} async-done(((bf16[8,16384]{1,0:T(8,128)(2,1)}), bf16[128,16384]{1,0:T(8,128)(2,1)}) %all-gather.2.cloned.1.call-update) | async-done | bytes 4194320 | tf_op jit(solution)/shard_map/all_gather | solution.py:62
  66.2 5.6 %fusion.30 = f32[128,176]{0,1:T(8,128)S(1)} fusion(bf16[128,16384]{1,0:T(8,128)(2,1)} %all-gather.2.cloned.1.call-done, bf16[176,16384]{1,0:T(8,128)(2,1)} %param.11), kind=kOutput, calls=%fused_computation.56 | convolution fusion | flops 738197504 | bytes 10051584 | tf_op jit(solution)/shard_map/dot_general | solution.py:65
  71.7 0.3 fusion.29
  72.1 31.1 %pmax.7 = f32[128]{0:T(128)S(1)} all-reduce(f32[128]{0:T(128)S(1)} %get-tuple-element.16), channel_id=1, replica_groups=mesh['groups'=2,'orient'=8,'img'=2] {'orient','img'}, use_global_device_ids=true, to_apply=%region_1.2 | all-reduce | flops 128 | bytes 1024 | tf_op jit(solution)/shard_map/pmax | solution.py:71
  103.2 0.1 fusion.20
  103.3 0.0 copy-done.1
  103.3 0.3 fusion.19
  103.6 58.4 %all-reduce.2 = (f32[128]{0:T(128)S(1)}, f32[128,24]{1,0:T(8,128)S(1)}) all-reduce(f32[128]{0:T(128)S(1)} %fusion.20, f32[128,24]{1,0:T(8,128)S(1)} %fusion.19), channel_id=1, replica_groups=mesh['groups'=2,'orient'=8,'img'=2] {'orient','img'}, use_global_device_ids=true, to_apply=%region_3.4 | all-reduce | flops 3200 | bytes 25600 | tf_op jit(solution)/shard_map/psum | solution.py:73
  162.0 0.6 log_add_fusion
  162.6 0.8 fusion.23
  163.4 0.7 dynamic-slice_divide_fusion
  164.1 6.4 %convolution_convert_fusion = bf16[176,16384]{1,0:T(8,128)(2,1)} fusion(bf16[128,176]{0,1:T(8,128)(2,1)S(1)} %divide_convert_fusion, bf16[128,16384]{1,0:T(8,128)(2,1)} %all-gather.2.cloned.1.call-done), kind=kOutput, calls=%fused_computation.1 | convolution fusion | flops 741081088 | bytes 10006528 | tf_op jit(solution)/shard_map/dot_general | solution.py:81
  (6 shorter events, 0.0 us)
Async XLA Ops:
  7.2 26.1 %copy-start = (f32[8,8192]{1,0:T(8,128)S(1)}, f32[8,8192]{1,0:T(8,128)}, u32[]{:S(2)}) copy-start(f32[8,8192]{1,0:T(8,128)} %param.15) | copy-start | bytes 786436
  7.2 59.0 %all-gather.2.cloned.1.call-start = ((), (), s32[]{:S(2)}) async-start(), calls=%async_computation | async-start | bytes 4456448 | tf_op jit(solution)/shard_map/all_gather | solution.py:62
  39.8 63.5 %copy-start.1 = (s32[176]{0:T(256)S(1)}, s32[176]{0:T(256)}, u32[]{:S(2)}) copy-start(s32[176]{0:T(256)} %param.12) | copy-start | bytes 2116
Sparse Core Ops, SparseCore 0:
  12.7 53.4 all-gather.1
where the time goes:
time: 178 us; the launch traced here: 177 us
  blocking collectives  103 us (58%)
  waiting for transfers between devices  26.4 us (15%)
  matrix products  21.4 us (12%)
  between operations  15.4 us (9%)
  other arithmetic  5.59 us (3%)
  local copies, waits for them, and re-layouts  5.06 us (3%)
    psum x1, blocking collectives, body(): totals = lax.psum(jnp.sum(exponent, axis=1), ('orient', 'img'))  58.4 us
    pmax x1, blocking collectives, body(): maxima = lax.pmax(jnp.max(scores, axis=1), ('orient', 'img'))  31.1 us
    all_gather x1, waiting for transfers between devices, body(): lax.all_gather(prepared, ('orient', 'img'), axis=0, tiled=True)  26.4 us
    unnamed x1, blocking collectives  13.9 us
    dot_general x1, matrix products, body(): per_group = jnp.dot(squared_ctf, powers.T, precision=lax.Precision.HIGHEST)  6.56 us
    dot_general x1, matrix products, body(): lax.dot_general(weights, gathered, (((0,), (0,)), ((), ())), preferred_el...  6.37 us
    dot_general x1, matrix products, body(): lax.dot_general(gathered, projections, (((1,), (1,)), ((), ())), preferre...  5.56 us
  transfers between devices with their start and end apart: 1, of which 1 were waited for; matrix products, arithmetic and copies ran while one was open for 7% of the time, Pallas kernels for 0%

commit v1 on v0

v1 whole, which is shorter than its diff:
```python
import functools
import math

import jax
import jax.numpy as jnp
from jax import lax
from jax.experimental import pallas as pl
from jax.experimental.pallas import tpu as pltpu
from jax.sharding import PartitionSpec as P

KY = 128
KX = 64
HALF = 8192
BOX = 128
LANES = 128
PIECES = 2
CHUNK = 1024
TILE = 1024
STEP = 2.0 * math.pi / BOX
MESH = pl.DeviceIdType.MESH
NT = (((1,), (1,)), ((), ()))
TN = (((0,), (0,)), ((), ()))


def split3(x):
    hi = x.astype(jnp.bfloat16)
    rest = x - hi.astype(jnp.float32)
    mid = rest.astype(jnp.bfloat16)
    low = (rest - mid.astype(jnp.float32)).astype(jnp.bfloat16)
    return hi, mid, low


def dot32(a, b, dims):
    return lax.dot_general(a, b, dims, preferred_element_type=jnp.float32)


def gather_kernel(
    n_orient,
    n_img,
    rows,
    images,
    shift,
    group,
    proj_hbm,
    slice_class,
    slice_angle,
    prior_hbm,
    ctf,
    g_out,
    w_out,
    mass_out,
    cls_out,
    lev_out,
    proj,
    prior,
    gat,
    scores,
    per_group,
    stat_src,
    stat_dst,
    own_src,
    own_dst,
    load_sem,
    ring_send,
    ring_recv,
    sib_send,
    sib_recv,
    out_sem,
    stat_send,
    stat_recv,
    own_send,
    own_recv,
):
    n_dev = n_orient * n_img
    n_all = n_dev * rows
    n_proj = proj.shape[0]
    n_cls, n_ang = prior.shape
    half_ring = n_orient // 2
    orient = lax.axis_index("orient")
    core = lax.axis_index("img")
    me = orient * n_img + core

    if n_orient == 8:
        spot = orient // 2 + (orient % 2) * (7 - 2 * (orient // 2))

        def orient_at(q):
            return 2 * (q % 4 + (q // 4) * (3 - 2 * (q % 4))) + q // 4

    else:
        spot = orient

        def orient_at(q):
            return q

    def chip(delta):
        return orient_at((spot + delta + n_orient) % n_orient)

    barrier = pltpu.get_barrier_semaphore()
    for r in range(1, n_dev):
        other = (me + r) % n_dev
        pl.semaphore_signal(
            barrier,
            inc=1,
            device_id={"orient": other // n_img, "img": other % n_img},
            device_id_type=MESH,
        )
    load_proj = pltpu.make_async_copy(proj_hbm, proj, load_sem.at[0])
    load_prior = pltpu.make_async_copy(prior_hbm, prior, load_sem.at[1])
    load_proj.start()
    load_prior.start()

    tx = shift[:, 0:1]
    ty = shift[:, 1:2]
    lane = lax.broadcasted_iota(jnp.int32, (rows, CHUNK), 1)
    inner = (tx * (lane % KX) + ty * (lane // KX)) & (BOX - 1)
    inner = inner.astype(jnp.float32) * STEP
    cos_in, sin_in = jnp.cos(inner), jnp.sin(inner)
    groups = group[...]
    reps = CHUNK // LANES

    def prepare(j, carry):
        start = pl.multiple_of(j * CHUNK, CHUNK)
        outer = (ty * (j * (CHUNK // KX) - KY // 2)) & (BOX - 1)
        outer = jnp.broadcast_to(outer, (rows, LANES)).astype(jnp.float32) * STEP
        cos_o = jnp.concatenate([jnp.cos(outer)] * reps, axis=1)
        sin_o = jnp.concatenate([jnp.sin(outer)] * reps, axis=1)
        cosine = cos_o * cos_in - sin_o * sin_in
        sine = sin_o * cos_in + cos_o * sin_in
        g = jnp.zeros((rows, CHUNK), jnp.float32)
        for h in range(ctf.shape[0]):
            g = jnp.where(groups == h, ctf[h : h + 1, pl.ds(start, CHUNK)], g)
        a = images[:, pl.ds(start, CHUNK)].astype(jnp.float32)
        b = images[:, pl.ds(pl.multiple_of(HALF + start, CHUNK), CHUNK)].astype(jnp.float32)
        moved = jnp.concatenate([g * (a * cosine + b * sine), g * (b * cosine - a * sine)], axis=0)
        gat[me, :, pl.ds(start, CHUNK)] = moved.astype(jnp.bfloat16)
        return carry

    lax.fori_loop(0, HALF // CHUNK, prepare, 0)
    tag = jnp.broadcast_to(groups.astype(jnp.float32), (rows, LANES))
    gat[me, :, HALF : HALF + LANES] = jnp.concatenate([tag, tag], axis=0).astype(jnp.bfloat16)

    width = HALF // PIECES
    length = (half_ring - 1) * PIECES + PIECES // 2

    def piece_of(direction, k):
        return (k % PIECES + direction * (PIECES // 2)) % PIECES

    def columns(p):
        return pl.ds(p * width, width + (LANES if p == PIECES - 1 else 0))

    def ring_copy(direction, k):
        step = k // PIECES
        source = chip(-step if direction == 0 else step) * n_img + core
        block = gat.at[source, :, columns(piece_of(direction, k))]
        return pltpu.make_async_remote_copy(
            src_ref=block,
            dst_ref=block,
            send_sem=ring_send.at[direction, k],
            recv_sem=ring_recv.at[direction, k],
            device_id={"orient": chip(1 if direction == 0 else -1), "img": core},
            device_id_type=MESH,
        )

    def ring_arrival(direction, k):
        step = 1 + k // PIECES
        source = chip(-step if direction == 0 else step) * n_img + core
        block = gat.at[source, :, columns(piece_of(direction, k))]
        return pltpu.make_async_remote_copy(
            src_ref=block,
            dst_ref=block,
            send_sem=ring_send.at[direction, k],
            recv_sem=ring_recv.at[direction, k],
            device_id={"orient": chip(1 if direction == 0 else -1), "img": core},
            device_id_type=MESH,
        )

    def sib_copy(index, delta, p, side):
        source = chip(delta) * n_img + (core if side == 0 else 1 - core)
        block = gat.at[source, :, columns(p)]
        return pltpu.make_async_remote_copy(
            src_ref=block,
            dst_ref=block,
            send_sem=sib_send.at[index],
            recv_sem=sib_recv.at[index],
            device_id={"orient": orient, "img": 1 - core},
            device_id_type=MESH,
        )

    def sib_args(direction, k):
        step = 1 + k // PIECES
        return (
            PIECES + 2 * k + direction,
            -step if direction == 0 else step,
            piece_of(direction, k),
        )

    pl.semaphore_wait(barrier, n_dev - 1)
    for k in range(PIECES):
        for direction in range(2):
            ring_copy(direction, k).start()
    for p in range(PIECES):
        sib_copy(p, 0, p, 0).start()

    def power_chunks(first, last):
        def step(j, acc):
            start = pl.multiple_of(j * 512, 512)
            re = proj[:, pl.ds(start, 512)].astype(jnp.float32)
            im = proj[:, pl.ds(pl.multiple_of(HALF + start, 512), 512)].astype(jnp.float32)
            parts = split3(re * re + im * im)
            table = ctf[:, pl.ds(start, 512)]
            t_hi, t_mid, t_low = split3(table * table)
            pair = jnp.concatenate(
                [t_hi.astype(jnp.float32), t_mid.astype(jnp.float32), t_low.astype(jnp.float32)], 0
            ).astype(jnp.bfloat16)
            for part in parts:
                acc = acc + dot32(pair, part, NT)
            return acc

        acc = jnp.zeros((3 * ctf.shape[0], n_proj), jnp.float32)
        acc = lax.fori_loop(first, last, step, acc)
        n = ctf.shape[0]
        total = acc[:n] + acc[n : 2 * n] + acc[2 * n :]
        per_group[...] = total if first == 0 else per_group[...] + total

    classes = slice_class[...]
    angles = slice_angle[...]

    def prior_row():
        hot = (lax.broadcasted_iota(jnp.int32, (n_ang, n_proj), 0) == angles).astype(jnp.float32)
        hot = hot.astype(jnp.bfloat16)
        total = jnp.zeros((n_cls, n_proj), jnp.float32)
        for part in split3(prior[...]):
            total = total + lax.dot_general(
                part, hot, (((1,), (0,)), ((), ())), preferred_element_type=jnp.float32
            )
        own = lax.broadcasted_iota(jnp.int32, (n_cls, n_proj), 0) == classes
        return jnp.sum(jnp.where(own, total, 0.0), axis=0, keepdims=True)

    def score(blocks, first, last, fresh):
        def step(j, carry):
            start = pl.multiple_of(j * 512, 512)
            left = jnp.concatenate([gat[d, :, pl.ds(start, 512)] for d in blocks], axis=0)
            re = proj[:, pl.ds(start, 512)]
            im = proj[:, pl.ds(pl.multiple_of(HALF + start, 512), 512)]
            return carry[0] + dot32(left, re, NT), carry[1] + dot32(left, im, NT)

        zero = jnp.zeros((len(blocks) * 2 * rows, n_proj), jnp.float32)
        a, b = lax.fori_loop(first, last, step, (zero, zero))
        for i, d in enumerate(blocks):
            base = 2 * rows * i
            part = a[base : base + rows] + b[base + rows : base + 2 * rows]
            scores[d] = part if fresh else scores[d] + part

    def both(delta):
        return [chip(delta) * n_img, chip(delta) * n_img + 1]

    out_copies = []

    def put_out(blocks):
        for d in blocks:
            copy = pltpu.make_async_copy(gat.at[d], g_out.at[d], out_sem.at[len(out_copies)])
            copy.start()
            out_copies.append(copy)

    n_power = HALF // 512
    for k in range(length):
        for direction in range(2):
            ring_arrival(direction, k).wait_recv()
            ahead = k + PIECES
            if ahead < length:
                ring_copy(direction, ahead).start()
            index, delta, p = sib_args(direction, k)
            sib_copy(index, delta, p, 0).start()
        if k == 0:
            load_proj.wait()
            load_prior.wait()
            prior_here = prior_row()
            power_chunks(0, n_power // 2)
        if k == 1:
            power_chunks(n_power // 2, n_power)
        if k == 2:
            for q in range(PIECES):
                sib_copy(q, 0, q, 1).wait_recv()
            score(both(0), 0, HALF // 512, True)
            put_out(both(0))
        if k >= PIECES and k % PIECES == min(1, PIECES - 1):
            step = k // PIECES
            for q in range((step - 1) * PIECES, step * PIECES):
                for direction in range(2):
                    index, delta, p = sib_args(direction, q)
                    sib_copy(index, delta, p, 1).wait_recv()
            blocks = both(-step) + both(step)
            score(blocks, 0, HALF // 512, True)
            put_out(blocks)

    step = half_ring - 1
    if (half_ring - 1) * PIECES + min(1, PIECES - 1) >= length:
        for q in range((step - 1) * PIECES, step * PIECES):
            for direction in range(2):
                index, delta, p = sib_args(direction, q)
                sib_copy(index, delta, p, 1).wait_recv()
        blocks = both(-step) + both(step)
        score(blocks, 0, HALF // 512, True)
        put_out(blocks)
    blocks = both(half_ring)
    for k in range((half_ring - 1) * PIECES, length):
        for direction in range(2):
            index, delta, p = sib_args(direction, k)
            sib_copy(index, delta, p, 1).wait_recv()
    score(blocks, 0, HALF // 512, True)
    put_out(blocks)

    tags = gat[:, :, HALF : HALF + LANES].astype(jnp.float32)
    tags = tags[:, :rows, :].reshape(n_all, LANES)
    tag_col = tags[:, 0:1]
    full = scores[...].reshape(n_all, n_proj)
    energy = jnp.zeros((n_all, n_proj), jnp.float32)
    for h in range(ctf.shape[0]):
        energy = jnp.where(tag_col == h, per_group[h : h + 1, :], energy)
    full = full - 0.5 * energy + prior_here
    top = jnp.max(full, axis=1, keepdims=True)
    expo = jnp.exp(full - top)
    slot = lax.broadcasted_iota(jnp.int32, (LANES, n_proj), 0)
    hot = jnp.where(slot == n_cls, 1.0, jnp.where(slot == classes, 1.0, 0.0)).astype(jnp.bfloat16)
    mass = jnp.zeros((n_all, LANES), jnp.float32)
    for part in split3(expo):
        mass = mass + dot32(part, hot, NT)
    mass = jnp.where(lax.broadcasted_iota(jnp.int32, (n_all, LANES), 1) == n_cls + 1, top, mass)
    turned = mass.T
    stat_src[...] = turned[n_cls : n_cls + 2, :]
    own_src[...] = mass.reshape(n_dev, rows, LANES)

    def stat_copy(r):
        other = (me + r) % n_dev
        return pltpu.make_async_remote_copy(
            src_ref=stat_src,
            dst_ref=stat_dst.at[me],
            send_sem=stat_send.at[r],
            recv_sem=stat_recv.at[r],
            device_id={"orient": other // n_img, "img": other % n_img},
            device_id_type=MESH,
        )

    def own_copy(r):
        other = (me + r) % n_dev
        return pltpu.make_async_remote_copy(
            src_ref=own_src.at[other],
            dst_ref=own_dst.at[me],
            send_sem=own_send.at[r],
            recv_sem=own_recv.at[r],
            device_id={"orient": other // n_img, "img": other % n_img},
            device_id_type=MESH,
        )

    def stat_arrival(r):
        source = (me - r + n_dev) % n_dev
        return pltpu.make_async_remote_copy(
            src_ref=stat_src,
            dst_ref=stat_dst.at[source],
            send_sem=stat_send.at[r],
            recv_sem=stat_recv.at[r],
            device_id={"orient": source // n_img, "img": source % n_img},
            device_id_type=MESH,
        )

    def own_arrival(r):
        source = (me - r + n_dev) % n_dev
        return pltpu.make_async_remote_copy(
            src_ref=own_src.at[source],
            dst_ref=own_dst.at[source],
            send_sem=own_send.at[r],
            recv_sem=own_recv.at[r],
            device_id={"orient": source // n_img, "img": source % n_img},
            device_id_type=MESH,
        )

    for r in range(1, n_dev):
        stat_copy(r).start()
    for r in range(1, n_dev):
        own_copy(r).start()
    stat_dst[me] = stat_src[...]
    own_dst[me] = own_src[me]
    for r in range(1, n_dev):
        stat_arrival(r).wait_recv()
    best = stat_dst[0, 1:2, :]
    for d in range(1, n_dev):
        best = jnp.maximum(best, stat_dst[d, 1:2, :])
    total = jnp.zeros_like(best)
    for d in range(n_dev):
        total = total + jnp.exp(stat_dst[d, 1:2, :] - best) * stat_dst[d, 0:1, :]
    factor = jnp.exp(stat_src[1:2, :] - best) / total
    factor = jnp.broadcast_to(factor, (LANES, n_all)).T[:, 0:1]
    weights = (expo * factor).astype(jnp.bfloat16)
    spread_r = lax.broadcasted_iota(jnp.int32, (n_all, 2 * n_all), 0)
    spread_c = lax.broadcasted_iota(jnp.int32, (n_all, 2 * n_all), 1)
    place = 2 * rows * (spread_r // rows) + spread_r % rows
    for part in range(2):
        spread = jnp.where(spread_c == place + part * rows, 1.0, 0.0).astype(jnp.bfloat16)
        w_out[part] = dot32(weights, spread, TN).astype(jnp.bfloat16)
    lanes = lax.broadcasted_iota(jnp.int32, (n_all, LANES), 1).astype(jnp.float32)
    member = jnp.where(tags == lanes, 1.0, 0.0).astype(jnp.bfloat16)
    mass_out[...] = dot32(member, weights, TN)[: ctf.shape[0]]

    for r in range(1, n_dev):
        own_arrival(r).wait_recv()
    best = own_dst[0, :, n_cls + 1 : n_cls + 2]
    for d in range(1, n_dev):
        best = jnp.maximum(best, own_dst[d, :, n_cls + 1 : n_cls + 2])
    sums = jnp.zeros((rows, LANES), jnp.float32)
    for d in range(n_dev):
        sums = sums + jnp.exp(own_dst[d, :, n_cls + 1 : n_cls + 2] - best) * own_dst[d]
    total = sums[:, n_cls : n_cls + 1]
    cls_out[...] = sums[:, :n_cls] / total
    lev_out[...] = best + jnp.log(total)

    for direction in range(2):
        for k in range(length):
            ring_copy(direction, k).wait_send()
            index, delta, p = sib_args(direction, k)
            sib_copy(index, delta, p, 0).wait_send()
    for p in range(PIECES):
        sib_copy(p, 0, p, 0).wait_send()
    for r in range(1, n_dev):
        stat_copy(r).wait_send()
        own_copy(r).wait_send()
    for copy in out_copies:
        copy.wait()


def sum_kernel(g_ref, w_ref, mass_ref, cls_ref, lev_ref, out_ref, mass_out, cls_out, lev_out):
    part = pl.program_id(1)

    @pl.when((pl.program_id(0) == 0) & (part == 0))
    def _():
        mass_out[...] = mass_ref[...]
        cls_out[...] = cls_ref[...]
        lev_out[...] = lev_ref[...]

    g = g_ref[...].reshape(w_ref.shape[2], out_ref.shape[1])
    out_ref[...] = jnp.dot(w_ref[part], g, preferred_element_type=jnp.float32).astype(jnp.bfloat16)


def body(
    n_orient,
    n_img,
    images,
    image_shift,
    image_group,
    projections,
    slice_class,
    slice_angle,
    log_prior,
    ctf_table,
):
    n_dev = n_orient * n_img
    rows = images.shape[0]
    n_all = n_dev * rows
    n_proj, feat = projections.shape
    n_grp = ctf_table.shape[0]
    n_cls = log_prior.shape[0]
    length = (n_orient // 2 - 1) * PIECES + PIECES // 2
    vmem = pl.BlockSpec(memory_space=pltpu.VMEM)
    hbm = pl.BlockSpec(memory_space=pl.ANY)
    f32, bf16 = jnp.float32, jnp.bfloat16
    dma = pltpu.SemaphoreType.DMA
    g, w, mass, cls, lev = pl.pallas_call(
        functools.partial(gather_kernel, n_orient, n_img, rows),
        out_shape=(
            jax.ShapeDtypeStruct((n_dev, 2 * rows, HALF + LANES), bf16),
            jax.ShapeDtypeStruct((2, n_proj, 2 * n_all), bf16),
            jax.ShapeDtypeStruct((n_grp, n_proj), f32),
            jax.ShapeDtypeStruct((rows, n_cls), f32),
            jax.ShapeDtypeStruct((rows, 1), f32),
        ),
        in_specs=[vmem, vmem, vmem, hbm, vmem, vmem, hbm, vmem],
        out_specs=(hbm, vmem, vmem, vmem, vmem),
        scratch_shapes=[
            pltpu.VMEM((n_proj, feat), bf16),
            pltpu.VMEM(log_prior.shape, f32),
            pltpu.VMEM((n_dev, 2 * rows, HALF + LANES), bf16),
            pltpu.VMEM((n_dev, rows, n_proj), f32),
            pltpu.VMEM((n_grp, n_proj), f32),
            pltpu.VMEM((2, n_all), f32),
            pltpu.VMEM((n_dev, 2, n_all), f32),
            pltpu.VMEM((n_dev, rows, LANES), f32),
            pltpu.VMEM((n_dev, rows, LANES), f32),
            dma((2,)),
            dma((2, length)),
            dma((2, length)),
            dma((2 * length + PIECES,)),
            dma((2 * length + PIECES,)),
            dma((n_dev,)),
            dma((n_dev,)),
            dma((n_dev,)),
            dma((n_dev,)),
            dma((n_dev,)),
        ],
        compiler_params=pltpu.CompilerParams(
            collective_id=0, has_side_effects=True, vmem_limit_bytes=48 * 2**20
        ),
    )(
        images,
        image_shift,
        image_group.reshape(rows, 1),
        projections,
        slice_class.reshape(1, n_proj),
        slice_angle.reshape(1, n_proj),
        log_prior,
        ctf_table,
    )
    tiles = HALF // TILE
    once = lambda shape: pl.BlockSpec(shape, lambda j, part: (0,) * len(shape))
    out, mass, cls, lev = pl.pallas_call(
        sum_kernel,
        grid=(tiles, 2),
        out_shape=(
            jax.ShapeDtypeStruct((n_proj, feat), bf16),
            jax.ShapeDtypeStruct(mass.shape, f32),
            jax.ShapeDtypeStruct(cls.shape, f32),
            jax.ShapeDtypeStruct(lev.shape, f32),
        ),
        in_specs=[
            pl.BlockSpec((n_dev, 2 * rows, TILE), lambda j, part: (0, 0, j)),
            once(w.shape),
            once(mass.shape),
            once(cls.shape),
            once(lev.shape),
        ],
        out_specs=(
            pl.BlockSpec((n_proj, TILE), lambda j, part: (0, part * tiles + j)),
            once(mass.shape),
            once(cls.shape),
            once(lev.shape),
        ),
        compiler_params=pltpu.CompilerParams(vmem_limit_bytes=48 * 2**20),
    )(g, w, mass, cls, lev)
    return out, mass, cls, lev.reshape(rows)


def solution(mesh):
    in_specs = (
        P(("groups", "orient", "img"), None),
        P(("groups", "orient", "img"), None),
        P(("groups", "orient", "img")),
        P(("orient", "img"), None),
        P(("orient", "img")),
        P(("orient", "img")),
        P(),
        P(),
    )
    out_specs = (
        P(("groups", "orient", "img"), None),
        P(None, ("groups", "orient", "img")),
        P(("groups", "orient", "img"), None),
        P(("groups", "orient", "img")),
    )
    return jax.shard_map(
        functools.partial(body, mesh.shape["orient"], mesh.shape["img"]),
        mesh=mesh,
        in_specs=in_specs,
        out_specs=out_specs,
        check_vma=False,
    )
```

time: 178 us -> 59.1 us (0.33)
  blocking collectives: 103 us -> 0 us
  Pallas kernels: 0 us -> 51.8 us
  waiting for transfers between devices: 26.4 us -> 0 us
  matrix products: 21.4 us -> 0 us
  between operations: 15.4 us -> 0.65 us
  other arithmetic: 5.59 us -> 0.63 us
    psum x1 -> x0, blocking collectives: 58.4 us -> none  [body(): totals = lax.psum(jnp.sum(exponent, axis=1), ('orient', 'img'))]
    pallas_call x0 -> x2, Pallas kernels: none -> 51.8 us  [the longest x1 43 us: body(): pl.pallas_call(functools.partial(gather_kernel, n_orient, n_img, rows), o...]
    pmax x1 -> x0, blocking collectives: 31.1 us -> none  [body(): maxima = lax.pmax(jnp.max(scores, axis=1), ('orient', 'img'))]
    all_gather x1 -> x0, waiting for transfers between devices: 26.4 us -> none  [body(): lax.all_gather(prepared, ('orient', 'img'), axis=0, tiled=True)]
    dot_general x7 -> x0, matrix products: 21.4 us -> none  [the longest x1 6.56 us: body(): per_group = jnp.dot(squared_ctf, powers.T, precision=lax.Precision.HIGHEST)]
    unnamed x1 -> x0, blocking collectives: 13.9 us -> none
    unnamed x7 -> x11, local copies, waits for them, and re-layouts: 2.21 us -> 5.02 us
    cos x1 -> x0, other arithmetic: 1.9 us -> none  [prepare_rows(): cosine = jnp.cos(phases)]
  transfers between devices with their start and end apart: 1 -> 0, of which waited for: 1 -> 0; matrix products, arithmetic and copies ran while one was open for 7% -> 0% of each run, Pallas kernels for 0% -> 0%
where the time goes in v1:
time: 59.1 us; the launch traced here: 58.8 us
  Pallas kernels  51.8 us (88%)
  local copies, waits for them, and re-layouts  5.75 us (10%)
  between operations  0.65 us (1%)
  other arithmetic  0.63 us (1%)
    pallas_call x1, Pallas kernels, body(): pl.pallas_call(functools.partial(gather_kernel, n_orient, n_img, rows), o...  43 us
    pallas_call x1, Pallas kernels, body(): pl.pallas_call(sum_kernel, grid=(tiles, 2), out_shape=(jax.ShapeDtypeStru...  8.81 us
    unnamed x11, local copies, waits for them, and re-layouts  5.02 us

profile of v1, /device:TPU:0, one launch (start us, length us, event | category | flops | bytes accessed | tf_op | source)
XLA Modules:
  0.0 58.8 jit_solution(9590652981361258292)
XLA Ops:
  0.6 0.8 %copy.14.shift = s32[8,2]{1,0:T(8,128)S(1)} copy(s32[8,2]{0,1:T(2,128)} %param.9) | data formatting | bytes 128 | tf_op args[1]
  1.4 0.7 %copy.15.group = s32[8,1]{1,0:T(8,128)S(1)} copy(s32[8,1]{0,1:T(1,128)} %bitcast.5) | data formatting | bytes 64 | tf_op jit(solution)/shard_map/reshape | solution.py:504
  2.1 0.0 copy-start
  2.1 1.0 %copy-done = f32[24,4608]{1,0:T(8,128)S(1)} copy-done((f32[24,4608]{1,0:T(8,128)S(1)}, f32[24,4608]{1,0:T(8,128)}, u32[]{:S(2)}) %copy-start) | copy-done | bytes 442392
  3.1 0.0 copy-start.1
  3.1 0.9 %copy-done.1 = bf16[8,16384]{1,0:T(8,128)(2,1)S(1)} copy-done((bf16[8,16384]{1,0:T(8,128)(2,1)S(1)}, bf16[8,16384]{1,0:T(8,128)(2,1)}, u32[]{:S(2)}) %copy-start.1) | copy-done | bytes 262168
  4.1 0.0 copy-start.2
  4.1 0.9 %copy-done.2 = f32[8,8192]{1,0:T(8,128)S(1)} copy-done((f32[8,8192]{1,0:T(8,128)S(1)}, f32[8,8192]{1,0:T(8,128)}, u32[]{:S(2)}) %copy-start.2) | copy-done | bytes 262168
  5.0 0.0 copy-start.3
  5.0 0.7 %copy-done.3 = s32[176]{0:T(256)S(1)} copy-done((s32[176]{0:T(256)S(1)}, s32[176]{0:T(256)}, u32[]{:S(2)}) %copy-start.3) | copy-done | bytes 728
  5.7 0.0 copy-start.4
  5.7 0.7 %copy-done.4 = s32[176]{0:T(256)S(1)} copy-done((s32[176]{0:T(256)S(1)}, s32[176]{0:T(256)}, u32[]{:S(2)}) %copy-start.4) | copy-done | bytes 728
  6.4 43.0 %shard_map.111 = (bf16[16,16,8320]{2,1,0:T(8,128)(2,1)S(1)}, bf16[2,176,256]{2,1,0:T(8,128)(2,1)S(1)}, f32[8,176]{1,0:T(8,128)S(1)}, f32[8,24]{1,0:T(8,128)S(1)}, f32[8,1]{1,0:T(8,128)S(1)}) custom-call(bf16[8,16384]{1,0:T(8,128)(2,1)S(1)} %copy-done.1, s32[8,2]{1,0:T(8,128)S(1)} %copy.14.shift, s32[8,1]{1,0:T(8,128)S(1)} %copy.15.group, ...), custom_call_target="tpu_custom_call" | custom-call | tf_op jit(solution)/shard_map/pallas_call | solution.py:466
  49.4 8.8 %shard_map.112 = (bf16[176,16384]{1,0:T(8,128)(2,1)}, f32[8,176]{1,0:T(8,128)}, f32[8,24]{1,0:T(8,128)}, f32[8,1]{1,0:T(8,128)S(1)}) custom-call(bf16[16,16,8320]{2,1,0:T(8,128)(2,1)S(1)} %get-tuple-element.13.g_ref, bf16[2,176,256]{2,1,0:T(8,128)(2,1)S(1)} %get-tuple-element.14.w_ref, f32[8,176]{1,0:T(8,128)S(1)} %get-tuple-element.15.mass_ref, ...), custom_call_target="tpu_custom_call" | custom-call | tf_op jit(solution)/shard_map/pallas_call | solution.py:513
  58.2 0.6 %reduce = f32[8]{0:T(128)} reduce(f32[8,1]{1,0:T(8,128)S(1)} %get-tuple-element.21, f32[]{:T(128)} %constant.3), dimensions={1}, to_apply=%get-tuple-element.21.reduce_sub_computation | reduce | bytes 68 | tf_op jit(solution)/shard_map/pallas_call | solution.py:513
Async XLA Ops:
  2.1 1.0 %copy-start = (f32[24,4608]{1,0:T(8,128)S(1)}, f32[24,4608]{1,0:T(8,128)}, u32[]{:S(2)}) copy-start(f32[24,4608]{1,0:T(8,128)} %prior_hbm.1) | copy-start | bytes 1327108
  3.1 0.9 %copy-start.1 = (bf16[8,16384]{1,0:T(8,128)(2,1)S(1)}, bf16[8,16384]{1,0:T(8,128)(2,1)}, u32[]{:S(2)}) copy-start(bf16[8,16384]{1,0:T(8,128)(2,1)} %images.1) | copy-start | bytes 786436
  4.1 0.9 %copy-start.2 = (f32[8,8192]{1,0:T(8,128)S(1)}, f32[8,8192]{1,0:T(8,128)}, u32[]{:S(2)}) copy-start(f32[8,8192]{1,0:T(8,128)} %ctf.1) | copy-start | bytes 786436
  5.0 0.7 %copy-start.3 = (s32[176]{0:T(256)S(1)}, s32[176]{0:T(256)}, u32[]{:S(2)}) copy-start(s32[176]{0:T(256)} %param.12) | copy-start | bytes 2116
  5.7 0.7 %copy-start.4 = (s32[176]{0:T(256)S(1)}, s32[176]{0:T(256)}, u32[]{:S(2)}) copy-start(s32[176]{0:T(256)} %param.13) | copy-start | bytes 2116

commit v2 on v1

--- a/solution.py
+++ b/solution.py
@@ -13,9 +13,10 @@
 HALF = 8192
 BOX = 128
 LANES = 128
-PIECES = 2
+PIECES = 4
 CHUNK = 1024
-TILE = 1024
+TILE = 2048
+VMEM_BYTES = 64 * 2**20
 STEP = 2.0 * math.pi / BOX
 MESH = pl.DeviceIdType.MESH
 NT = (((1,), (1,)), ((), ()))
@@ -38,21 +39,27 @@
     n_orient,
     n_img,
     rows,
-    images,
-    shift,
-    group,
+    images_hbm,
+    shift_hbm,
+    group_hbm,
     proj_hbm,
-    slice_class,
-    slice_angle,
+    class_hbm,
+    angle_hbm,
     prior_hbm,
-    ctf,
+    ctf_hbm,
     g_out,
     w_out,
     mass_out,
     cls_out,
     lev_out,
+    images,
+    shift_row,
+    group_row,
     proj,
+    slice_class,
+    slice_angle,
     prior,
+    ctf,
     gat,
     scores,
     per_group,
@@ -104,18 +111,40 @@
             device_id={"orient": other // n_img, "img": other % n_img},
             device_id_type=MESH,
         )
-    load_proj = pltpu.make_async_copy(proj_hbm, proj, load_sem.at[0])
-    load_prior = pltpu.make_async_copy(prior_hbm, prior, load_sem.at[1])
-    load_proj.start()
-    load_prior.start()
-
-    tx = shift[:, 0:1]
-    ty = shift[:, 1:2]
+    loads = [
+        pltpu.make_async_copy(source, place, load_sem.at[i])
+        for i, (source, place) in enumerate(
+            (
+                (shift_hbm, shift_row),
+                (group_hbm, group_row),
+                (ctf_hbm, ctf),
+                (images_hbm, images),
+                (class_hbm, slice_class),
+                (angle_hbm, slice_angle),
+                (prior_hbm, prior),
+                (proj_hbm, proj),
+            )
+        )
+    ]
+    for load in loads:
+        load.start()
+    diagonal = lax.broadcasted_iota(jnp.int32, (rows, rows), 0) == lax.broadcasted_iota(
+        jnp.int32, (rows, rows), 1
+    )
+
+    def column(row):
+        return jnp.sum(jnp.where(diagonal, row, 0.0), axis=1, keepdims=True)
+
+    for load in loads[:4]:
+        load.wait()
+
+    tx = column(shift_row[0:1, :].astype(jnp.float32)).astype(jnp.int32)
+    ty = column(shift_row[1:2, :].astype(jnp.float32)).astype(jnp.int32)
     lane = lax.broadcasted_iota(jnp.int32, (rows, CHUNK), 1)
     inner = (tx * (lane % KX) + ty * (lane // KX)) & (BOX - 1)
     inner = inner.astype(jnp.float32) * STEP
     cos_in, sin_in = jnp.cos(inner), jnp.sin(inner)
-    groups = group[...]
+    groups = column(group_row[...].astype(jnp.float32)).astype(jnp.int32)
     reps = CHUNK // LANES
 
     def prepare(j, carry):
@@ -222,9 +251,6 @@
         total = acc[:n] + acc[n : 2 * n] + acc[2 * n :]
         per_group[...] = total if first == 0 else per_group[...] + total
 
-    classes = slice_class[...]
-    angles = slice_angle[...]
-
     def prior_row():
         hot = (lax.broadcasted_iota(jnp.int32, (n_ang, n_proj), 0) == angles).astype(jnp.float32)
         hot = hot.astype(jnp.bfloat16)
@@ -236,16 +262,13 @@
         own = lax.broadcasted_iota(jnp.int32, (n_cls, n_proj), 0) == classes
         return jnp.sum(jnp.where(own, total, 0.0), axis=0, keepdims=True)
 
-    def score(blocks, first, last, fresh):
-        def step(j, carry):
-            start = pl.multiple_of(j * 512, 512)
-            left = jnp.concatenate([gat[d, :, pl.ds(start, 512)] for d in blocks], axis=0)
-            re = proj[:, pl.ds(start, 512)]
-            im = proj[:, pl.ds(pl.multiple_of(HALF + start, 512), 512)]
-            return carry[0] + dot32(left, re, NT), carry[1] + dot32(left, im, NT)
-
-        zero = jnp.zeros((len(blocks) * 2 * rows, n_proj), jnp.float32)
-        a, b = lax.fori_loop(first, last, step, (zero, zero))
+    def score(blocks, pieces, fresh):
+        a = jnp.zeros((len(blocks) * 2 * rows, n_proj), jnp.float32)
+        b = a
+        for p in pieces:
+            left = jnp.concatenate([gat[d, :, p * width : (p + 1) * width] for d in blocks], axis=0)
+            a = a + dot32(left, proj[:, p * width : (p + 1) * width], NT)
+            b = b + dot32(left, proj[:, HALF + p * width : HALF + (p + 1) * width], NT)
         for i, d in enumerate(blocks):
             base = 2 * rows * i
             part = a[base : base + rows] + b[base + rows : base + 2 * rows]
@@ -262,6 +285,14 @@
             copy.start()
             out_copies.append(copy)
 
+    def await_sib(first, end):
+        for q in range(first, end):
+            for direction in range(2):
+                index, delta, p = sib_args(direction, q)
+                sib_copy(index, delta, p, 1).wait_recv()
+
+    early, late = (0, 2), (1, 3)
+    last = half_ring - 1
     n_power = HALF // 512
     for k in range(length):
         for direction in range(2):
@@ -272,43 +303,36 @@
             index, delta, p = sib_args(direction, k)
             sib_copy(index, delta, p, 0).start()
         if k == 0:
-            load_proj.wait()
-            load_prior.wait()
+            for load in loads[4:]:
+                load.wait()
+            classes = slice_class[...]
+            angles = slice_angle[...]
             prior_here = prior_row()
-            power_chunks(0, n_power // 2)
-        if k == 1:
-            power_chunks(n_power // 2, n_power)
-        if k == 2:
-            for q in range(PIECES):
-                sib_copy(q, 0, q, 1).wait_recv()
-            score(both(0), 0, HALF // 512, True)
-            put_out(both(0))
-        if k >= PIECES and k % PIECES == min(1, PIECES - 1):
-            step = k // PIECES
-            for q in range((step - 1) * PIECES, step * PIECES):
-                for direction in range(2):
-                    index, delta, p = sib_args(direction, q)
-                    sib_copy(index, delta, p, 1).wait_recv()
+        elif k <= 4:
+            power_chunks((k - 1) * n_power // 4, k * n_power // 4)
+        step = (k - 1) // PIECES
+        if k % PIECES == 1 and 1 <= step < last:
+            await_sib(step * PIECES - PIECES, step * PIECES)
             blocks = both(-step) + both(step)
-            score(blocks, 0, HALF // 512, True)
+            if step == 1:
+                for q in range(PIECES):
+                    sib_copy(q, 0, q, 1).wait_recv()
+                blocks = both(0) + blocks
+            score(blocks, early, True)
             put_out(blocks)
-
-    step = half_ring - 1
-    if (half_ring - 1) * PIECES + min(1, PIECES - 1) >= length:
-        for q in range((step - 1) * PIECES, step * PIECES):
-            for direction in range(2):
-                index, delta, p = sib_args(direction, q)
-                sib_copy(index, delta, p, 1).wait_recv()
-        blocks = both(-step) + both(step)
-        score(blocks, 0, HALF // 512, True)
-        put_out(blocks)
-    blocks = both(half_ring)
-    for k in range((half_ring - 1) * PIECES, length):
-        for direction in range(2):
-            index, delta, p = sib_args(direction, k)
-            sib_copy(index, delta, p, 1).wait_recv()
-    score(blocks, 0, HALF // 512, True)
-    put_out(blocks)
+        if k % PIECES == 2 and 1 <= step < last:
+            score(blocks, late, False)
+        if k == last * PIECES:
+            await_sib(k - PIECES, k)
+            blocks = both(-last) + both(last)
+            score(blocks, early, True)
+            put_out(blocks)
+    await_sib(last * PIECES, length - 1)
+    score(both(half_ring), early, True)
+    await_sib(length - 1, length)
+    blocks = blocks + both(half_ring)
+    put_out(both(half_ring))
+    score(blocks, late, False)
 
     tags = gat[:, :, HALF : HALF + LANES].astype(jnp.float32)
     tags = tags[:, :rows, :].reshape(n_all, LANES)
@@ -411,7 +435,8 @@
         sums = sums + jnp.exp(own_dst[d, :, n_cls + 1 : n_cls + 2] - best) * own_dst[d]
     total = sums[:, n_cls : n_cls + 1]
     cls_out[...] = sums[:, :n_cls] / total
-    lev_out[...] = best + jnp.log(total)
+    evidence = best + jnp.log(total)
+    lev_out[...] = jnp.sum(jnp.where(diagonal, evidence, 0.0), axis=0, keepdims=True)
 
     for direction in range(2):
         for k in range(length):
@@ -427,17 +452,32 @@
         copy.wait()
 
 
-def sum_kernel(g_ref, w_ref, mass_ref, cls_ref, lev_ref, out_ref, mass_out, cls_out, lev_out):
-    part = pl.program_id(1)
-
-    @pl.when((pl.program_id(0) == 0) & (part == 0))
-    def _():
-        mass_out[...] = mass_ref[...]
-        cls_out[...] = cls_ref[...]
-        lev_out[...] = lev_ref[...]
-
-    g = g_ref[...].reshape(w_ref.shape[2], out_ref.shape[1])
-    out_ref[...] = jnp.dot(w_ref[part], g, preferred_element_type=jnp.float32).astype(jnp.bfloat16)
+def sum_kernel(
+    g_hbm, w, mass_ref, cls_ref, lev_ref, out, mass_out, cls_out, lev_out, g, held, g_sems, sems
+):
+    n_proj = out.shape[0]
+    weights = w[...].reshape(2 * n_proj, w.shape[2])
+    loads = []
+    for j in range(HALF // TILE):
+        at = pl.ds(j * TILE, TILE)
+        loads.append(pltpu.make_async_copy(g_hbm.at[:, :, at], g.at[:, :, at], g_sems.at[j]))
+        loads[-1].start()
+    copies = []
+    for j in range(HALF // TILE):
+        loads[j].wait()
+        block = g[:, :, j * TILE : (j + 1) * TILE].reshape(w.shape[2], TILE)
+        sums = jnp.dot(weights, block, preferred_element_type=jnp.float32).astype(jnp.bfloat16)
+        for part in range(2):
+            at = pl.ds(part * HALF + j * TILE, TILE)
+            held[:, at] = sums[part * n_proj : (part + 1) * n_proj]
+            copy = pltpu.make_async_copy(held.at[:, at], out.at[:, at], sems.at[2 * j + part])
+            copy.start()
+            copies.append(copy)
+    mass_out[...] = mass_ref[...]
+    cls_out[...] = cls_ref[...]
+    lev_out[...] = lev_ref[...]
+    for copy in copies:
+        copy.wait()
 
 
 def body(
@@ -460,7 +500,8 @@
     n_cls = log_prior.shape[0]
     length = (n_orient // 2 - 1) * PIECES + PIECES // 2
     vmem = pl.BlockSpec(memory_space=pltpu.VMEM)
-    hbm = pl.BlockSpec(memory_space=pl.ANY)
+    hbm = pl.BlockSpec(memory_space=pltpu.HBM)
+    i32 = jnp.int32
     f32, bf16 = jnp.float32, jnp.bfloat16
     dma = pltpu.SemaphoreType.DMA
     g, w, mass, cls, lev = pl.pallas_call(
@@ -470,13 +511,19 @@
             jax.ShapeDtypeStruct((2, n_proj, 2 * n_all), bf16),
             jax.ShapeDtypeStruct((n_grp, n_proj), f32),
             jax.ShapeDtypeStruct((rows, n_cls), f32),
-            jax.ShapeDtypeStruct((rows, 1), f32),
+            jax.ShapeDtypeStruct((1, rows), f32),
         ),
-        in_specs=[vmem, vmem, vmem, hbm, vmem, vmem, hbm, vmem],
+        in_specs=[hbm] * 8,
         out_specs=(hbm, vmem, vmem, vmem, vmem),
         scratch_shapes=[
+            pltpu.VMEM(images.shape, bf16),
+            pltpu.VMEM((2, rows), i32),
+            pltpu.VMEM((1, rows), i32),
             pltpu.VMEM((n_proj, feat), bf16),
+            pltpu.VMEM((1, n_proj), i32),
+            pltpu.VMEM((1, n_proj), i32),
             pltpu.VMEM(log_prior.shape, f32),
+            pltpu.VMEM(ctf_table.shape, f32),
             pltpu.VMEM((n_dev, 2 * rows, HALF + LANES), bf16),
             pltpu.VMEM((n_dev, rows, n_proj), f32),
             pltpu.VMEM((n_grp, n_proj), f32),
@@ -484,7 +531,7 @@
             pltpu.VMEM((n_dev, 2, n_all), f32),
             pltpu.VMEM((n_dev, rows, LANES), f32),
             pltpu.VMEM((n_dev, rows, LANES), f32),
-            dma((2,)),
+            dma((8,)),
             dma((2, length)),
             dma((2, length)),
             dma((2 * length + PIECES,)),
@@ -496,43 +543,35 @@
             dma((n_dev,)),
         ],
         compiler_params=pltpu.CompilerParams(
-            collective_id=0, has_side_effects=True, vmem_limit_bytes=48 * 2**20
+            collective_id=0, has_side_effects=True, vmem_limit_bytes=VMEM_BYTES
         ),
     )(
         images,
-        image_shift,
-        image_group.reshape(rows, 1),
+        image_shift.T,
+        image_group.reshape(1, rows),
         projections,
         slice_class.reshape(1, n_proj),
         slice_angle.reshape(1, n_proj),
         log_prior,
         ctf_table,
     )
-    tiles = HALF // TILE
-    once = lambda shape: pl.BlockSpec(shape, lambda j, part: (0,) * len(shape))
     out, mass, cls, lev = pl.pallas_call(
         sum_kernel,
-        grid=(tiles, 2),
         out_shape=(
             jax.ShapeDtypeStruct((n_proj, feat), bf16),
             jax.ShapeDtypeStruct(mass.shape, f32),
             jax.ShapeDtypeStruct(cls.shape, f32),
             jax.ShapeDtypeStruct(lev.shape, f32),
         ),
-        in_specs=[
-            pl.BlockSpec((n_dev, 2 * rows, TILE), lambda j, part: (0, 0, j)),
-            once(w.shape),
-            once(mass.shape),
-            once(cls.shape),
-            once(lev.shape),
+        in_specs=[hbm, vmem, vmem, vmem, vmem],
+        out_specs=(hbm, vmem, vmem, vmem),
+        scratch_shapes=[
+            pltpu.VMEM((n_dev, 2 * rows, HALF), bf16),
+            pltpu.VMEM((n_proj, feat), bf16),
+            dma((HALF // TILE,)),
+            dma((2 * (HALF // TILE),)),
         ],
-        out_specs=(
-            pl.BlockSpec((n_proj, TILE), lambda j, part: (0, part * tiles + j)),
-            once(mass.shape),
-            once(cls.shape),
-            once(lev.shape),
-        ),
-        compiler_params=pltpu.CompilerParams(vmem_limit_bytes=48 * 2**20),
+        compiler_params=pltpu.CompilerParams(vmem_limit_bytes=VMEM_BYTES),
     )(g, w, mass, cls, lev)
     return out, mass, cls, lev.reshape(rows)
 

time: 59.1 us -> 44.4 us (0.75)
  Pallas kernels: 51.8 us -> 43.6 us
  local copies, waits for them, and re-layouts: 5.75 us -> 0 us
  other arithmetic: 0.63 us -> 0 us
    pallas_call x1, Pallas kernels: 43 us -> 37.5 us  [body(): pl.pallas_call(functools.partial(gather_kernel, n_orient, n_img, rows), o...]
    unnamed x11 -> x0, local copies, waits for them, and re-layouts: 5.02 us -> none
    pallas_call x1, Pallas kernels: 8.81 us -> 6.13 us  [body(): pl.pallas_call(sum_kernel, out_shape=(jax.ShapeDtypeStruct((n_proj, feat)...]
    reshape x1 -> x0, local copies, waits for them, and re-layouts: 0.73 us -> none  [body(): image_group.reshape(rows, 1)]
    pallas_call x1 -> x0, other arithmetic: 0.63 us -> none  [body(): pl.pallas_call(sum_kernel, grid=(tiles, 2), out_shape=(jax.ShapeDtypeStru...]
where the time goes in v2:
time: 44.4 us; the launch traced here: 44.3 us
  Pallas kernels  43.6 us (98%)
  between operations  0.64 us (1%)
    pallas_call x1, Pallas kernels, body(): pl.pallas_call(functools.partial(gather_kernel, n_orient, n_img, rows), o...  37.5 us
    pallas_call x1, Pallas kernels, body(): pl.pallas_call(sum_kernel, out_shape=(jax.ShapeDtypeStruct((n_proj, feat)...  6.13 us

profile of v2, /device:TPU:0, one launch (start us, length us, event | category | flops | bytes accessed | tf_op | source)
XLA Modules:
  0.0 44.3 jit_solution(16520684048803810263)
XLA Ops:
  0.6 37.5 %shard_map.111 = (bf16[16,16,8320]{2,1,0:T(8,128)(2,1)}, bf16[2,176,256]{2,1,0:T(8,128)(2,1)}, f32[8,176]{1,0:T(8,128)}, f32[8,24]{1,0:T(8,128)}, f32[1,8]{1,0:T(1,128)}) custom-call(bf16[8,16384]{1,0:T(8,128)(2,1)} %images_hbm.1, s32[2,8]{1,0:T(2,128)} %bitcast.5, s32[1,8]{1,0:T(1,128)} %bitcast.8, bf16[176,16384]{1,0:T(8,128)(2,1)} %proj_hbm.1, ...), custom_call_target="tpu_custom_call" | custom-call | tf_op jit(solution)/shard_map/pallas_call | solution.py:507
  38.1 6.1 %shard_map.112 = (bf16[176,16384]{1,0:T(8,128)(2,1)}, f32[8,176]{1,0:T(8,128)}, f32[8,24]{1,0:T(8,128)}, f32[1,8]{1,0:T(1,128)}) custom-call(bf16[16,16,8320]{2,1,0:T(8,128)(2,1)} %get-tuple-element.13.g_hbm, bf16[2,176,256]{2,1,0:T(8,128)(2,1)} %get-tuple-element.14.w, f32[8,176]{1,0:T(8,128)} %get-tuple-element.15.mass_ref, ...), custom_call_target="tpu_custom_call" | custom-call | tf_op jit(solution)/shard_map/pallas_call | solution.py:558
